TPU v7x, 32 devices: a whole 2x2x4 slice. The times are simulated.
32 devices in a mesh: grp: 2 (over x), samp: 4 (over y, core), col: 4 (over z).
Axes of the slice: x: 2, y: 2, z: 4, core: 2. Of those that a mesh axis runs over, the one named last changes fastest.
Arguments:
- dosage: bfloat16 [2048, 20480], P('samp', 'col'), may hold values from -6 to 6
- candidates: bfloat16 [2048, 16384], P('samp', 'col'), may hold values from -6 to 6
- traits: float32 [32, 2048], P('grp', 'samp'), parts along dimension 0, may hold values from -6 to 6
- coef_start: float32 [32, 20480], P('grp', 'col'), parts along dimension 0, may hold values from -0.0390625 to 0.0390625
- screened: int32 [1024], replicated, may hold values from 0 to 16383, as said below
- penalty: float32 [32], P('grp'), parts along dimension 0, may hold values from 0.002 to 0.05
Outputs:
- residual: float32 [32, 2048], P('grp', 'samp'), parts along dimension 0
- score: float32 [32, 16384], P('grp', 'col'), parts along dimension 0
There are 2 independent parts, one for each index of `grp`. A program takes and returns all parts, laid end to end along the dimension named above; an argument that names none is the same for every part. Nothing has to cross between parts.
Inputs may be any that keep to these rules, and one draw needn't show every extreme that they name: `screened`: entries are distinct. In each aligned block of 256 entries, at most 128 lie in one block of 4096 candidate indices, and exactly 128 in one such block.
All inputs are finite; a program needn't handle non-finite values.
Results may differ from a plain program's by a relative error of at most 0.008.
Values may be sent and summed in bfloat16 or wider, within the bound.
A program may use at most 64 MiB of HBM per device.

v0:
```python
import math

import jax
import jax.numpy as jnp
from jax import lax
from jax.sharding import PartitionSpec as P

NEW_DEV = 256
MOST = 128
CAND_DEV = 4096
ITERS = 2


def rows_dot(left, right):
    return lax.dot_general(
        left, right, (((1,), (1,)), ((), ())), preferred_element_type=jnp.float32
    )


def shrink(moved, threshold):
    return moved - jnp.clip(moved, -threshold, threshold)


def on_device(dosage, candidates, traits, coef_start, screened, penalty):
    col_count = lax.axis_size("col")
    samp_count = lax.axis_size("samp")
    col_index = lax.axis_index("col")
    sample_rows = dosage.shape[0]
    active_cols = dosage.shape[1]
    samples = sample_rows * samp_count
    total_cols = (active_cols + NEW_DEV) * col_count
    step_size = 1.0 / (1.0 + math.sqrt(total_cols / samples)) ** 2
    threshold = (step_size * penalty)[:, None]
    source = screened // CAND_DEV
    local_index = screened % CAND_DEV
    block_src = source.reshape(col_count, NEW_DEV)
    block_local = local_index.reshape(col_count, NEW_DEV)
    owned = block_src == col_index
    slot_order = jnp.argsort(jnp.where(owned, 0, 1), axis=1, stable=True)[:, :MOST]
    slot_live = jnp.take_along_axis(owned, slot_order, axis=1)
    slot_cols = jnp.where(slot_live, jnp.take_along_axis(block_local, slot_order, axis=1), 0)
    outgoing = jnp.take(candidates, slot_cols.reshape(-1), axis=1)
    outgoing = outgoing * slot_live.reshape(-1).astype(jnp.bfloat16)[None, :]
    outgoing = outgoing.reshape(sample_rows, col_count, MOST)
    arrived = lax.all_to_all(outgoing, "col", split_axis=1, concat_axis=1, tiled=True)
    mine_src = lax.dynamic_slice_in_dim(source, col_index * NEW_DEV, NEW_DEV)
    one_hot = (mine_src[:, None] == jnp.arange(col_count)[None, :]).astype(jnp.int32)
    slot_rank = jnp.sum(jnp.cumsum(one_hot, axis=0) * one_hot, axis=1) - 1
    admitted = jnp.take(
        arrived.reshape(sample_rows, col_count * MOST), mine_src * MOST + slot_rank, axis=1
    )
    keep_mask = jnp.ones((active_cols + NEW_DEV,), jnp.float32)
    extra_cols = admitted.shape[1]
    coef_now = jnp.concatenate(
        [coef_start, jnp.zeros((coef_start.shape[0], extra_cols), jnp.float32)], axis=1
    )

    def fitted_values(coef_now):
        coef_bf = coef_now.astype(jnp.bfloat16)
        partial_value = rows_dot(coef_bf[:, :active_cols], dosage) + rows_dot(
            coef_bf[:, active_cols:], admitted
        )
        return lax.psum(partial_value, "col")

    for sweep in range(ITERS):
        fitted = fitted_values(coef_now)
        resid_bf = (traits - fitted).astype(jnp.bfloat16)
        partial_value = jnp.concatenate(
            [
                jnp.dot(resid_bf, dosage, preferred_element_type=jnp.float32),
                jnp.dot(resid_bf, admitted, preferred_element_type=jnp.float32),
            ],
            axis=1,
        )
        gradient = lax.psum(partial_value, "samp") / samples
        coef_now = keep_mask[None, :] * shrink(coef_now + step_size * gradient, threshold)
    residual = traits - fitted_values(coef_now)
    resid_bf = residual.astype(jnp.bfloat16)
    score_part = jnp.dot(resid_bf, candidates, preferred_element_type=jnp.float32)
    score = lax.psum(score_part, "samp") / math.sqrt(samples)
    return (residual, score)


def solution(mesh):
    placed = (P("samp", "col"), P("samp", "col"), P("grp", "samp"), P("grp", "col"), P(), P("grp"))
    return jax.shard_map(
        on_device,
        mesh=mesh,
        in_specs=placed,
        out_specs=(P("grp", "samp"), P("grp", "col")),
        check_vma=False,
    )
```

profile of v0, /device:TPU:0, one launch (start us, length us, event | category | flops | bytes accessed | tf_op | source)
XLA Modules:
  0.0 237.2 jit_solution(16888679722558141531)
XLA Ops:
  10.0 1.2 reduce-window.6
  11.7 6.5 %copy.13 = bf16[512,4096]{0,1:T(8,128)(2,1)} copy(bf16[512,4096]{1,0:T(8,128)(2,1)} %param.7) | data formatting | bytes 8388608 | tf_op args[1]
  18.9 4.6 %gather_fusion.2 = pred[512]{0:T(512)(128)(4,1)S(1)} fusion(pred[4,256]{1,0:T(4,128)(4,1)S(1)} %eq.43, s32[512]{0:T(512)S(1)} %fusion.16), kind=kCustom, calls=%fused_computation.2 | custom fusion | bytes 5120 | tf_op jit(solution)/shard_map/jit(take_along_axis)/gather | solution.py:40
  24.2 4.8 %gather_fusion.3 = s32[512]{0:T(512)S(1)} fusion(s32[4,256]{1,0:T(4,128)S(1)} %reshape.139, s32[512]{0:T(512)S(1)} %fusion.16), kind=kCustom, calls=%fused_computation.3 | custom fusion | bytes 8192 | tf_op jit(solution)/shard_map/jit(take_along_axis)/gather | solution.py:41
  29.0 4.7 %gather_fusion = bf16[512,512]{1,0:T(8,128)(2,1)S(1)} fusion(bf16[512,4096]{0,1:T(8,128)(2,1)} %copy.13, s32[1024]{0:T(1024)S(1)} %pad_clamp_fusion.1), kind=kCustom, calls=%fused_computation | custom fusion | bytes 1050624 | tf_op jit(solution)/shard_map/jit(_take)/gather | solution.py:42
  33.8 1.0 select_multiply_fusion
  34.8 6.3 %all-to-all-start = ((bf16[512,4,128]{0,2,1:T(8,128)(2,1)}), bf16[512,4,128]{0,2,1:T(8,128)(2,1)S(1)}, u32[]{:S(2)}, u32[]{:S(2)}) async-start(bf16[512,4,128]{0,2,1:T(8,128)(2,1)} %select_multiply_fusion), calls=%async_computation | async-start | bytes 1048576 | tf_op jit(solution)/shard_map/all_to_all | solution.py:45
  41.1 14.4 %all-to-all-done = bf16[512,4,128]{0,2,1:T(8,128)(2,1)S(1)} async-done(((bf16[512,4,128]{0,2,1:T(8,128)(2,1)}), bf16[512,4,128]{0,2,1:T(8,128)(2,1)S(1)}, u32[]{:S(2)}, u32[]{:S(2)}) %all-to-all-start) | async-done | bytes 524320 | tf_op jit(solution)/shard_map/all_to_all | solution.py:45
  55.6 1.2 gather_fusion.1
  57.0 4.0 %convolution_add_fusion.2 = f32[16,512]{1,0:T(8,128)S(1)} fusion(f32[16,512]{1,0:T(8,128)S(1)} %fusion.9, bf16[512,5120]{1,0:T(8,128)(2,1)} %param.6, bf16[16,5376]{1,0:T(8,128)(2,1)S(1)} %pad_convert_fusion), kind=kOutput, calls=%fused_computation.6 | convolution fusion | flops 83894272 | bytes 5472256 | tf_op jit(solution)/shard_map/dot_general | solution.py:15
  60.9 17.1 %psum.42 = f32[16,512]{1,0:T(8,128)S(1)} all-reduce(f32[16,512]{1,0:T(8,128)S(1)} %convolution_add_fusion.2), channel_id=1, replica_groups=mesh['grp'=2,'samp'=4,'col'=4] {'col'}, use_global_device_ids=true, to_apply=%region_4.5 | all-reduce | flops 8192 | bytes 65536 | tf_op jit(solution)/shard_map/psum | solution.py:63
  78.1 3.3 %fusion.23 = f32[16,5120]{1,0:T(8,128)S(1)} fusion(bf16[16,512]{1,0:T(8,128)(2,1)S(1)} %subtract_convert_fusion.2, bf16[512,5120]{1,0:T(8,128)(2,1)} %param.6), kind=kOutput, calls=%fused_computation.64 | convolution fusion | flops 83886080 | bytes 5586944 | tf_op jit(solution)/shard_map/dot_general | solution.py:70
  82.5 30.5 %all-reduce.5.cloned.1.call-done = f32[16,5376]{1,0:T(8,128)} async-done(((f32[16,5376]{1,0:T(8,128)}), f32[16,5376]{1,0:T(8,128)}) %all-reduce.5.cloned.1.call-update) | async-done | bytes 344080 | tf_op jit(solution)/shard_map/psum | solution.py:75
  112.9 1.1 fusion.19
  114.2 4.0 %convolution_add_fusion.1 = f32[16,512]{1,0:T(8,128)S(1)} fusion(f32[16,512]{1,0:T(8,128)S(1)} %fusion.7, bf16[512,5120]{1,0:T(8,128)(2,1)} %param.6, bf16[16,5376]{1,0:T(8,128)(2,1)S(1)} %fusion.19), kind=kOutput, calls=%fused_computation.5 | convolution fusion | flops 83894272 | bytes 5472256 | tf_op jit(solution)/shard_map/dot_general | solution.py:15
  118.2 19.0 %psum.44 = f32[16,512]{1,0:T(8,128)S(1)} all-reduce(f32[16,512]{1,0:T(8,128)S(1)} %convolution_add_fusion.1), channel_id=1, replica_groups=mesh['grp'=2,'samp'=4,'col'=4] {'col'}, use_global_device_ids=true, to_apply=%region_6.7 | all-reduce | flops 8192 | bytes 65536 | tf_op jit(solution)/shard_map/psum | solution.py:63
  137.2 3.3 %fusion.24 = f32[16,5120]{1,0:T(8,128)S(1)} fusion(bf16[16,512]{1,0:T(8,128)(2,1)S(1)} %subtract_convert_fusion.1, bf16[512,5120]{1,0:T(8,128)(2,1)} %param.6), kind=kOutput, calls=%fused_computation.65 | convolution fusion | flops 83886080 | bytes 5586944 | tf_op jit(solution)/shard_map/dot_general | solution.py:70
  141.6 29.8 %all-reduce.7.cloned.1.call-done = f32[16,5376]{1,0:T(8,128)} async-done(((f32[16,5376]{1,0:T(8,128)}), f32[16,5376]{1,0:T(8,128)}) %all-reduce.7.cloned.1.call-update) | async-done | bytes 344080 | tf_op jit(solution)/shard_map/psum | solution.py:75
  171.4 1.1 subtract_convert_fusion
  172.8 3.9 %convolution_add_fusion = f32[16,512]{1,0:T(8,128)S(1)} fusion(f32[16,512]{1,0:T(8,128)S(1)} %fusion.5, bf16[512,5120]{1,0:T(8,128)(2,1)} %param.6, bf16[16,5376]{1,0:T(8,128)(2,1)S(1)} %subtract_convert_fusion), kind=kOutput, calls=%fused_computation.4 | convolution fusion | flops 83894272 | bytes 5472256 | tf_op jit(solution)/shard_map/dot_general | solution.py:15
  176.7 19.0 %psum.46 = f32[16,512]{1,0:T(8,128)S(1)} all-reduce(f32[16,512]{1,0:T(8,128)S(1)} %convolution_add_fusion), channel_id=1, replica_groups=mesh['grp'=2,'samp'=4,'col'=4] {'col'}, use_global_device_ids=true, to_apply=%region_8.9 | all-reduce | flops 8192 | bytes 65536 | tf_op jit(solution)/shard_map/psum | solution.py:63
  195.8 3.6 %fusion.3 = f32[16,4096]{1,0:T(8,128)} fusion(bf16[512,4096]{1,0:T(8,128)(2,1)} %param.7, f32[16,512]{1,0:T(8,128)S(1)} %sub.31), kind=kOutput, calls=%fused_computation.20 | convolution fusion | flops 67117056 | bytes 4489216 | tf_op jit(solution)/shard_map/dot_general | solution.py:79
  199.3 29.7 %all-reduce.9.cloned.1.call-done = f32[16,4096]{1,0:T(8,128)} async-done(((f32[16,4096]{1,0:T(8,128)}), f32[16,4096]{1,0:T(8,128)}) %all-reduce.9.cloned.1.call-update) | async-done | bytes 262160 | tf_op jit(solution)/shard_map/psum | solution.py:80
  229.0 1.7 broadcast_multiply_fusion
  (54 shorter events, 7.7 us)
Async XLA Ops:
  7.2 11.0 %sort.19.cloned.1.call-start = ((), (), s32[]{:S(2)}) async-start(), calls=%async_computation.4 | async-start | bytes 24608 | tf_op jit(solution)/shard_map/jit(argsort)/sort | solution.py:39
  18.2 22.9 %copy-start = (f32[16,5120]{1,0:T(8,128)S(1)}, f32[16,5120]{1,0:T(8,128)}, u32[]{:S(2)}) copy-start(f32[16,5120]{1,0:T(8,128)} %param.9) | copy-start | bytes 983044
  33.8 44.3 %copy-start.2 = (f32[16,512]{1,0:T(8,128)S(1)}, f32[16,512]{1,0:T(8,128)}, u32[]{:S(2)}) copy-start(f32[16,512]{1,0:T(8,128)} %param.8) | copy-start | bytes 98308
  34.8 20.8 %all-to-all-start = ((bf16[512,4,128]{0,2,1:T(8,128)(2,1)}), bf16[512,4,128]{0,2,1:T(8,128)(2,1)S(1)}, u32[]{:S(2)}, u32[]{:S(2)}) async-start(bf16[512,4,128]{0,2,1:T(8,128)(2,1)} %select_multiply_fusion), calls=%async_computation | async-start | bytes 1048576 | tf_op jit(solution)/shard_map/all_to_all | solution.py:45
  41.1 71.8 %all-reduce.5.cloned.1.call-start = ((), (), s32[]{:S(2)}) async-start(), calls=%async_computation.1 | async-start | bytes 688128 | tf_op jit(solution)/shard_map/psum | solution.py:75
  57.0 25.5 %copy-start.4 = (f32[16]{0:T(128)S(1)}, f32[16]{0:T(128)}, u32[]{:S(2)}) copy-start(f32[16]{0:T(128)} %param.11) | copy-start | bytes 196
  82.4 89.0 %all-reduce.7.cloned.1.call-start = ((), (), s32[]{:S(2)}) async-start(), calls=%async_computation.2 | async-start | bytes 688128 | tf_op jit(solution)/shard_map/psum | solution.py:75
  114.2 57.2 %copy-start.1 = (f32[16,5376]{1,0:T(8,128)S(1)}, f32[16,5376]{1,0:T(8,128)}, u32[]{:S(2)}) copy-start(f32[16,5376]{1,0:T(8,128)} %all-reduce.5.cloned.1.call-done) | copy-start | bytes 1032196
  141.6 87.4 %all-reduce.9.cloned.1.call-start = ((), (), s32[]{:S(2)}) async-start(), calls=%async_computation.3 | async-start | bytes 524288 | tf_op jit(solution)/shard_map/psum | solution.py:80
  195.7 35.0 %copy-start.3 = (f32[16,512]{1,0:T(8,128)}, f32[16,512]{1,0:T(8,128)S(1)}, u32[]{:S(2)}) copy-start(f32[16,512]{1,0:T(8,128)S(1)} %sub.31) | copy-start | bytes 98308
Sparse Core Ops, SparseCore 0:
  10.9 2.1 sort.21.cloned.1.call-done
  82.5 30.3 all-reduce.4
  141.7 29.6 all-reduce.6
  199.5 29.5 all-reduce.8
  (1 shorter events, 0.0 us)
where the time goes:
time: 238 us; the launch traced here: 237 us
  waiting for transfers between devices  104 us (44%)
  blocking collectives  55.1 us (23%)
  matrix products  23.2 us (10%)
  local copies, waits for them, and re-layouts  22.9 us (10%)
  between operations  13.9 us (6%)
  other arithmetic  11.3 us (5%)
  starting transfers between devices  6.41 us (3%)
    psum x2, waiting for transfers between devices, on_device(): gradient = lax.psum(partial_value, 'samp') / samples  60.2 us
    psum x3, blocking collectives, fitted_values(): return lax.psum(partial_value, 'col')  55.1 us
    psum x1, waiting for transfers between devices, on_device(): score = lax.psum(score_part, 'samp') / math.sqrt(samples)  29.7 us
    all_to_all x1, waiting for transfers between devices, on_device(): lax.all_to_all(outgoing, 'col', split_axis=1, concat_axis=1, tiled=True)  14.4 us
    dot_general x6, matrix products, rows_dot(): lax.dot_general(left, right, (((1,), (1,)), ((), ())), preferred_element_...  12.6 us
    dot_general x2, matrix products, on_device(): jnp.dot(resid_bf, dosage, preferred_element_type=jnp.float32)  6.56 us
    unnamed x12, local copies, waits for them, and re-layouts  6.5 us
    all_to_all x1, starting transfers between devices, on_device(): lax.all_to_all(outgoing, 'col', split_axis=1, concat_axis=1, tiled=True)  6.32 us
  transfers between devices with their start and end apart: 4, of which 4 were waited for; matrix products, arithmetic and copies ran while one was open for 0% of the time, Pallas kernels for 0%

commit v1 on v0

v1 whole, which is shorter than its diff:
```python
import functools
import math

import jax
import jax.numpy as jnp
from jax import lax
from jax.experimental import pallas as pl
from jax.experimental.pallas import tpu as pltpu
from jax.sharding import PartitionSpec as P

NEW_DEV = 256
MOST = 128
CAND_DEV = 4096
ITERS = 2
WIDE = 1024
LAG_A, LAG_B, LAG_C = 2, 4, 6

F32, BF16 = jnp.float32, jnp.bfloat16


def dot_nn(left, right):
    return jnp.dot(left, right, preferred_element_type=F32)


def dot_nt(left, right):
    return lax.dot_general(left, right, (((1,), (1,)), ((), ())), preferred_element_type=F32)


def kernel(
    sizes,
    dosage_hbm, cand_hbm, traits_hbm, coef_hbm, screened_hbm, penalty_hbm,
    resid_out, score_out,
    dosage, cand, traits, coef_start, screened, penalty,
    one_hot, admitted, coef_new, resid_f32, resid_bf, score_half,
    fit_slots, grad_bf, from_core, chip_sums, coef_bf,
    load_sem, cand_sem, small_sem, out_sem,
    fit_send, fit_recv, a_send, a_recv, b_send, b_recv, c_send, c_recv,
):
    n_col, n_samp, samples, step_size = sizes
    n_y = n_samp // 2
    col = lax.axis_index("col")
    samp = lax.axis_index("samp")
    core = lax.rem(samp, 2)
    other = 1 - core
    y_at = lax.div(samp, 2)
    core_peer = {"samp": y_at * 2 + other}
    y_peers = [{"samp": lax.rem(y_at + d, n_y) * 2 + core} for d in range(1, n_y)]
    col_peers = [{"col": lax.rem(col + d, n_col)} for d in range(1, n_col)]

    active = dosage.shape[1]
    slots = admitted.shape[1]
    n_dos = active // WIDE
    n_cand = CAND_DEV // WIDE

    loads = []
    for i in range(n_dos):
        at = (slice(None), pl.ds(i * WIDE, WIDE))
        loads.append(pltpu.make_async_copy(dosage_hbm.at[at], dosage.at[at], load_sem.at[i]))
    small = [
        pltpu.make_async_copy(src, dst, small_sem.at[i])
        for i, (src, dst) in enumerate(
            [(coef_hbm, coef_start), (traits_hbm, traits), (screened_hbm, screened), (penalty_hbm, penalty)]
        )
    ]
    cand_load = pltpu.make_async_copy(cand_hbm, cand, cand_sem.at[0])
    small[0].start()
    for copy in loads:
        copy.start()
    for copy in small[1:]:
        copy.start()
    cand_load.start()

    barrier = pltpu.get_barrier_semaphore()
    for peer in [core_peer] + y_peers + col_peers:
        pl.semaphore_signal(barrier, inc=1, device_id=peer, device_id_type=pl.DeviceIdType.MESH)

    sends = []

    def remote(src, dst, send_sem, recv_sem, peer):
        copy = pltpu.make_async_remote_copy(
            src_ref=src, dst_ref=dst, send_sem=send_sem, recv_sem=recv_sem,
            device_id=peer, device_id_type=pl.DeviceIdType.MESH,
        )
        copy.start()
        sends.append(copy)
        return copy

    def send_fit(turn, fitted):
        fit_slots[turn, col] = fitted.astype(BF16)
        return [
            remote(
                fit_slots.at[turn, col], fit_slots.at[turn, col],
                fit_send.at[turn, d], fit_recv.at[turn, d], peer,
            )
            for d, peer in enumerate(col_peers)
        ]

    def take_fit(turn, copies):
        for copy in copies:
            copy.wait_recv()
        total = fit_slots[turn, 0].astype(F32)
        for c in range(1, n_col):
            total = total + fit_slots[turn, c].astype(F32)
        resid_f32[...] = traits[...] - total
        resid_bf[...] = resid_f32[...].astype(BF16)

    small[0].wait()
    fitted = jnp.zeros(traits.shape, F32)
    for i in range(n_dos):
        loads[i].wait()
        at = slice(i * WIDE, (i + 1) * WIDE)
        fitted = fitted + dot_nt(coef_start[:, at].astype(BF16), dosage[:, at])
    pl.semaphore_wait(barrier, 1 + len(y_peers) + len(col_peers))
    fit_copies = send_fit(0, fitted)

    for copy in small[1:]:
        copy.wait()
    names = screened[...]
    local = names - col * CAND_DEV
    owned = (local >= 0) & (local < CAND_DEV)
    owned_f = jnp.where(owned, 1.0, 0.0)
    upper = (
        lax.broadcasted_iota(jnp.int32, (NEW_DEV, NEW_DEV), 0)
        <= lax.broadcasted_iota(jnp.int32, (NEW_DEV, NEW_DEV), 1)
    )
    rank = dot_nn(owned_f.astype(BF16), jnp.where(upper, 1.0, 0.0).astype(BF16)) * owned_f
    want = lax.broadcasted_iota(jnp.int32, (MOST, NEW_DEV), 0).astype(F32) + 1.0
    lanes = lax.broadcasted_iota(jnp.int32, (MOST, WIDE), 1).astype(F32)
    local_f = local.astype(F32) + 1.0
    for b in range(n_col):
        hit = rank[b : b + 1, :] == want
        column = jnp.sum(jnp.where(hit, local_f[b : b + 1, :], 0.0), axis=1, keepdims=True) - 1.0
        for i in range(n_cand):
            one_hot[b * MOST : (b + 1) * MOST, i * WIDE : (i + 1) * WIDE] = jnp.where(
                lanes == column - float(i * WIDE), 1.0, 0.0
            ).astype(BF16)
    cand_load.wait()
    for j in range(slots // 256):
        at = slice(j * 256, (j + 1) * 256)
        admitted[:, at] = dot_nt(cand[...], one_hot[at, :]).astype(BF16)

    threshold = step_size * penalty[...]
    scale = step_size / samples
    design = [(dosage, i * WIDE, WIDE) for i in range(n_dos)] + [(admitted, 0, slots)]
    tested = [(cand, i * WIDE, WIDE) for i in range(n_cand)]

    take_fit(0, fit_copies)

    for turn in range(ITERS + 1):
        last = turn == ITERS
        chunks = tested if last else design
        count = len(chunks)
        a_copies, b_copies, c_copies = {}, {}, {}
        fitted = jnp.zeros(traits.shape, F32)
        if last:
            out_copy = pltpu.make_async_copy(resid_f32, resid_out, out_sem.at[0])
            out_copy.start()
        outs = []
        resid = resid_bf[...]
        for t in range(count + LAG_C):
            if t < count:
                ref, start, width = chunks[t]
                half = width // 2
                part = dot_nn(resid, ref[:, start : start + width]).astype(BF16)
                grad_bf[turn, t, 0, :, :half] = part[:, :half]
                grad_bf[turn, t, 1, :, :half] = part[:, half:]
                a_copies[t] = remote(
                    grad_bf.at[turn, t, other, :, pl.ds(0, half)],
                    from_core.at[turn, t, :, pl.ds(0, half)],
                    a_send.at[turn, t], a_recv.at[turn, t], core_peer,
                )
            i = t - LAG_A
            if 0 <= i < count:
                half = chunks[i][2] // 2
                a_copies[i].wait_recv()
                chip_sum = grad_bf[turn, i, core, :, :half].astype(F32) + from_core[
                    turn, i, :, :half
                ].astype(F32)
                chip_sums[turn, i, y_at, :, :half] = chip_sum.astype(BF16)
                here = chip_sums.at[turn, i, y_at, :, pl.ds(0, half)]
                b_copies[i] = [
                    remote(here, here, b_send.at[turn, i, d], b_recv.at[turn, i, d], peer)
                    for d, peer in enumerate(y_peers)
                ]
            i = t - LAG_B
            if 0 <= i < count:
                ref, start, width = chunks[i]
                half = width // 2
                for copy in b_copies[i]:
                    copy.wait_recv()
                total = chip_sums[turn, i, 0, :, :half].astype(F32)
                for y in range(1, n_y):
                    total = total + chip_sums[turn, i, y, :, :half].astype(F32)
                if last:
                    score_half[i] = total * (1.0 / math.sqrt(samples))
                    here = score_out.at[:, pl.ds(pl.multiple_of(start + core * half, 128), half)]
                    copy = pltpu.make_async_copy(score_half.at[i], here, out_sem.at[1 + i])
                    copy.start()
                    outs.append(copy)
                    c_copies[i] = remote(
                        score_half.at[i], here, c_send.at[turn, i], c_recv.at[turn, i], core_peer
                    )
                else:
                    if turn > 0:
                        before = coef_new[i, :, :half]
                    elif ref is admitted:
                        before = jnp.zeros((traits.shape[0], half), F32)
                    else:
                        before = coef_start[:, pl.ds(pl.multiple_of(start + core * half, 128), half)]
                    moved = before + scale * total
                    after = moved - jnp.clip(moved, -threshold, threshold)
                    coef_new[i, :, :half] = after
                    coef_bf[turn, i, core, :, :half] = after.astype(BF16)
                    here = coef_bf.at[turn, i, core, :, pl.ds(0, half)]
                    c_copies[i] = remote(here, here, c_send.at[turn, i], c_recv.at[turn, i], core_peer)
            i = t - LAG_C
            if 0 <= i < count:
                ref, start, width = chunks[i]
                half = width // 2
                c_copies[i].wait_recv()
                if not last:
                    fitted = fitted + dot_nt(coef_bf[turn, i, 0, :, :half], ref[:, start : start + half])
                    fitted = fitted + dot_nt(
                        coef_bf[turn, i, 1, :, :half], ref[:, start + half : start + width]
                    )
        if not last:
            take_fit(turn + 1, send_fit(turn + 1, fitted))

    out_copy.wait()
    for copy in outs:
        copy.wait()
    for copy in sends:
        copy.wait_send()


def on_device(dosage, candidates, traits, coef_start, screened, penalty):
    n_col = lax.axis_size("col")
    n_samp = lax.axis_size("samp")
    rows, active = dosage.shape
    n_traits = traits.shape[0]
    samples = rows * n_samp
    total_cols = (active + NEW_DEV) * n_col
    step_size = 1.0 / (1.0 + math.sqrt(total_cols / samples)) ** 2
    slots = MOST * n_col
    chunks = active // WIDE + 1
    half = max(WIDE, slots) // 2
    turns = ITERS + 1
    n_y = n_samp // 2
    any_spec = pl.BlockSpec(memory_space=pl.ANY)
    dma = pltpu.SemaphoreType.DMA
    return pl.pallas_call(
        functools.partial(kernel, (n_col, n_samp, samples, step_size)),
        out_shape=(
            jax.ShapeDtypeStruct(traits.shape, F32),
            jax.ShapeDtypeStruct((n_traits, CAND_DEV), F32),
        ),
        in_specs=[any_spec] * 6,
        out_specs=(any_spec, any_spec),
        scratch_shapes=[
            pltpu.VMEM(dosage.shape, BF16),
            pltpu.VMEM(candidates.shape, BF16),
            pltpu.VMEM(traits.shape, F32),
            pltpu.VMEM(coef_start.shape, F32),
            pltpu.VMEM((n_col, NEW_DEV), jnp.int32),
            pltpu.VMEM((n_traits, 1), F32),
            pltpu.VMEM((slots, CAND_DEV), BF16),
            pltpu.VMEM((rows, slots), BF16),
            pltpu.VMEM((chunks, n_traits, half), F32),
            pltpu.VMEM(traits.shape, F32),
            pltpu.VMEM(traits.shape, BF16),
            pltpu.VMEM((CAND_DEV // WIDE, n_traits, WIDE // 2), F32),
            pltpu.VMEM((turns, n_col) + traits.shape, BF16),
            pltpu.VMEM((turns, chunks, 2, n_traits, half), BF16),
            pltpu.VMEM((turns, chunks, n_traits, half), BF16),
            pltpu.VMEM((turns, chunks, n_y, n_traits, half), BF16),
            pltpu.VMEM((ITERS, chunks, 2, n_traits, half), BF16),
            dma((active // WIDE,)),
            dma((1,)),
            dma((4,)),
            dma((1 + CAND_DEV // WIDE,)),
            dma((turns, n_col - 1)),
            dma((turns, n_col - 1)),
            dma((turns, chunks)),
            dma((turns, chunks)),
            dma((turns, chunks, n_y - 1)),
            dma((turns, chunks, n_y - 1)),
            dma((turns, chunks)),
            dma((turns, chunks)),
        ],
        compiler_params=pltpu.CompilerParams(
            collective_id=0, has_side_effects=True, vmem_limit_bytes=50 * 1024 * 1024
        ),
    )(
        dosage, candidates, traits, coef_start,
        screened.reshape(n_col, NEW_DEV), penalty.reshape(n_traits, 1),
    )


def solution(mesh):
    placed = (P("samp", "col"), P("samp", "col"), P("grp", "samp"), P("grp", "col"), P(), P("grp"))
    return jax.shard_map(
        on_device,
        mesh=mesh,
        in_specs=placed,
        out_specs=(P("grp", "samp"), P("grp", "col")),
        check_vma=False,
    )
```

time: 238 us -> 48.7 us (0.20)
  waiting for transfers between devices: 104 us -> 0 us
  blocking collectives: 55.1 us -> 0 us
  Pallas kernels: 0 us -> 43.3 us
  matrix products: 23.2 us -> 0 us
  local copies, waits for them, and re-layouts: 22.9 us -> 4.48 us
  between operations: 13.9 us -> 0.64 us
  other arithmetic: 11.3 us -> 0 us
  starting transfers between devices: 6.41 us -> 0 us
    psum x3 -> x0, waiting for transfers between devices: 89.9 us -> none  [the longest x2 60.2 us: on_device(): gradient = lax.psum(partial_value, 'samp') / samples]
    psum x3 -> x0, blocking collectives: 55.1 us -> none  [fitted_values(): return lax.psum(partial_value, 'col')]
    pallas_call x0 -> x1, Pallas kernels: none -> 43.3 us  [on_device(): pl.pallas_call(functools.partial(kernel, (n_col, n_samp, samples, step_si...]
    dot_general x11 -> x0, matrix products: 23.2 us -> none  [the longest x6 12.6 us: rows_dot(): lax.dot_general(left, right, (((1,), (1,)), ((), ())), preferred_element_...]
    gather x4 -> x0, local copies, waits for them, and re-layouts: 15.3 us -> none  [the longest x1 4.83 us: on_device(): jnp.take_along_axis(block_local, slot_order, axis=1)]
    all_to_all x1 -> x0, waiting for transfers between devices: 14.4 us -> none  [on_device(): lax.all_to_all(outgoing, 'col', split_axis=1, concat_axis=1, tiled=True)]
    all_to_all x1 -> x0, starting transfers between devices: 6.32 us -> none  [on_device(): lax.all_to_all(outgoing, 'col', split_axis=1, concat_axis=1, tiled=True)]
    unnamed x12 -> x6, local copies, waits for them, and re-layouts: 6.5 us -> 3.05 us
  transfers between devices with their start and end apart: 4 -> 0, of which waited for: 4 -> 0; matrix products, arithmetic and copies ran while one was open for 0% -> 0% of each run, Pallas kernels for 0% -> 0%
where the time goes in v1:
time: 48.7 us; the launch traced here: 48.4 us
  Pallas kernels  43.3 us (89%)
  local copies, waits for them, and re-layouts  4.48 us (9%)
  between operations  0.64 us (1%)
    pallas_call x1, Pallas kernels, on_device(): pl.pallas_call(functools.partial(kernel, (n_col, n_samp, samples, step_si...  43.3 us
    unnamed x6, local copies, waits for them, and re-layouts  3.05 us

profile of v1, /device:TPU:0, one launch (start us, length us, event | category | flops | bytes accessed | tf_op | source)
XLA Modules:
  0.0 48.4 jit_solution(695475551662481597)
XLA Ops:
  0.6 0.7 %reshape.10.screened_hbm = s32[4,256]{1,0:T(4,128)S(1)} reshape(s32[1024]{0:T(1024)} %param.10) | data formatting | bytes 8192 | tf_op jit(solution)/shard_map/reshape | solution.py:295
  1.3 0.7 %copy.8.penalty_hbm = f32[16,1]{1,0:T(8,128)S(1)} copy(f32[16,1]{0,1:T(1,128)} %bitcast.1) | data formatting | bytes 128 | tf_op jit(solution)/shard_map/reshape | solution.py:295
  2.1 0.0 copy-start
  2.1 1.0 %copy-done = f32[16,5120]{1,0:T(8,128)S(1)} copy-done((f32[16,5120]{1,0:T(8,128)S(1)}, f32[16,5120]{1,0:T(8,128)}, u32[]{:S(2)}) %copy-start) | copy-done | bytes 327704
  3.0 0.0 copy-start.1
  3.0 0.8 %copy-done.1 = f32[16,512]{1,0:T(8,128)S(1)} copy-done((f32[16,512]{1,0:T(8,128)S(1)}, f32[16,512]{1,0:T(8,128)}, u32[]{:S(2)}) %copy-start.1) | copy-done | bytes 32792
  3.8 43.3 %shard_map.77 = (f32[16,512]{1,0:T(8,128)S(1)}, f32[16,4096]{1,0:T(8,128)S(1)}) custom-call(bf16[512,5120]{1,0:T(8,128)(2,1)} %dosage_hbm.1, bf16[512,4096]{1,0:T(8,128)(2,1)} %cand_hbm.1, f32[16,512]{1,0:T(8,128)S(1)} %copy-done.1, f32[16,5120]{1,0:T(8,128)S(1)} %copy-done, s32[4,256]{1,0:T(4,128)S(1)} %reshape.10.screened_hbm, f32[16,1]{1,0:T(8,128)S(1)} %copy.8.penalty_hbm), custom_call_target="tpu_custom_call" | custom-call | tf_op jit(solution)/shard_map/pallas_call | solution.py:251
  47.1 0.6 %copy.11 = f32[16,512]{1,0:T(8,128)} copy(f32[16,512]{1,0:T(8,128)S(1)} %get-tuple-element.4) | data formatting | bytes 65536
  47.7 0.7 %copy.12 = f32[16,4096]{1,0:T(8,128)} copy(f32[16,4096]{1,0:T(8,128)S(1)} %get-tuple-element.5) | data formatting | bytes 524288
Async XLA Ops:
  2.1 1.0 %copy-start = (f32[16,5120]{1,0:T(8,128)S(1)}, f32[16,5120]{1,0:T(8,128)}, u32[]{:S(2)}) copy-start(f32[16,5120]{1,0:T(8,128)} %coef_hbm.1) | copy-start | bytes 983044
  3.0 0.8 %copy-start.1 = (f32[16,512]{1,0:T(8,128)S(1)}, f32[16,512]{1,0:T(8,128)}, u32[]{:S(2)}) copy-start(f32[16,512]{1,0:T(8,128)} %traits_hbm.1) | copy-start | bytes 98308

commit v2 on v1

--- a/solution.py
+++ b/solution.py
@@ -13,7 +13,6 @@
 CAND_DEV = 4096
 ITERS = 2
 WIDE = 1024
-LAG_A, LAG_B, LAG_C = 2, 4, 6
 
 F32, BF16 = jnp.float32, jnp.bfloat16
 
@@ -31,7 +30,7 @@
     dosage_hbm, cand_hbm, traits_hbm, coef_hbm, screened_hbm, penalty_hbm,
     resid_out, score_out,
     dosage, cand, traits, coef_start, screened, penalty,
-    one_hot, admitted, coef_new, resid_f32, resid_bf, score_half,
+    one_hot, admitted, coef_new, resid_f32, resid_bf, sent, score_half,
     fit_slots, grad_bf, from_core, chip_sums, coef_bf,
     load_sem, cand_sem, small_sem, out_sem,
     fit_send, fit_recv, a_send, a_recv, b_send, b_recv, c_send, c_recv,
@@ -86,7 +85,9 @@
         return copy
 
     def send_fit(turn, fitted):
-        fit_slots[turn, col] = fitted.astype(BF16)
+        change = (fitted if turn == 0 else fitted - sent[...]).astype(BF16)
+        sent[...] = change.astype(F32) if turn == 0 else sent[...] + change.astype(F32)
+        fit_slots[turn, col] = change
         return [
             remote(
                 fit_slots.at[turn, col], fit_slots.at[turn, col],
@@ -101,8 +102,9 @@
         total = fit_slots[turn, 0].astype(F32)
         for c in range(1, n_col):
             total = total + fit_slots[turn, c].astype(F32)
-        resid_f32[...] = traits[...] - total
-        resid_bf[...] = resid_f32[...].astype(BF16)
+        resid = (traits if turn == 0 else resid_f32)[...] - total
+        resid_f32[...] = resid
+        resid_bf[...] = resid.astype(BF16)
 
     small[0].wait()
     fitted = jnp.zeros(traits.shape, F32)
@@ -115,7 +117,9 @@
 
     for copy in small[1:]:
         copy.wait()
-    names = screened[...]
+    names = jnp.concatenate(
+        [screened[pl.ds(b * NEW_DEV, NEW_DEV)].reshape(1, NEW_DEV) for b in range(n_col)], axis=0
+    )
     local = names - col * CAND_DEV
     owned = (local >= 0) & (local < CAND_DEV)
     owned_f = jnp.where(owned, 1.0, 0.0)
@@ -139,7 +143,12 @@
         at = slice(j * 256, (j + 1) * 256)
         admitted[:, at] = dot_nt(cand[...], one_hot[at, :]).astype(BF16)
 
-    threshold = step_size * penalty[...]
+    n_traits = traits.shape[0]
+    same = lax.broadcasted_iota(jnp.int32, (n_traits, n_traits), 0) == lax.broadcasted_iota(
+        jnp.int32, (n_traits, n_traits), 1
+    )
+    penalty_row = penalty[...].reshape(1, n_traits)
+    threshold = step_size * jnp.sum(jnp.where(same, penalty_row, 0.0), axis=1, keepdims=True)
     scale = step_size / samples
     design = [(dosage, i * WIDE, WIDE) for i in range(n_dos)] + [(admitted, 0, slots)]
     tested = [(cand, i * WIDE, WIDE) for i in range(n_cand)]
@@ -157,72 +166,68 @@
             out_copy.start()
         outs = []
         resid = resid_bf[...]
-        for t in range(count + LAG_C):
-            if t < count:
-                ref, start, width = chunks[t]
-                half = width // 2
-                part = dot_nn(resid, ref[:, start : start + width]).astype(BF16)
-                grad_bf[turn, t, 0, :, :half] = part[:, :half]
-                grad_bf[turn, t, 1, :, :half] = part[:, half:]
-                a_copies[t] = remote(
-                    grad_bf.at[turn, t, other, :, pl.ds(0, half)],
-                    from_core.at[turn, t, :, pl.ds(0, half)],
-                    a_send.at[turn, t], a_recv.at[turn, t], core_peer,
+        for t in range(count):
+            ref, start, width = chunks[t]
+            half = width // 2
+            part = dot_nn(resid, ref[:, start : start + width]).astype(BF16)
+            grad_bf[turn, t, 0, :, :half] = part[:, :half]
+            grad_bf[turn, t, 1, :, :half] = part[:, half:]
+            a_copies[t] = remote(
+                grad_bf.at[turn, t, other, :, pl.ds(0, half)],
+                from_core.at[turn, t, :, pl.ds(0, half)],
+                a_send.at[turn, t], a_recv.at[turn, t], core_peer,
+            )
+        for i in range(count):
+            half = chunks[i][2] // 2
+            a_copies[i].wait_recv()
+            chip_sum = grad_bf[turn, i, core, :, :half].astype(F32) + from_core[
+                turn, i, :, :half
+            ].astype(F32)
+            chip_sums[turn, i, y_at, :, :half] = chip_sum.astype(BF16)
+            here = chip_sums.at[turn, i, y_at, :, pl.ds(0, half)]
+            b_copies[i] = [
+                remote(here, here, b_send.at[turn, i, d], b_recv.at[turn, i, d], peer)
+                for d, peer in enumerate(y_peers)
+            ]
+        for i in range(count):
+            ref, start, width = chunks[i]
+            half = width // 2
+            for copy in b_copies[i]:
+                copy.wait_recv()
+            total = chip_sums[turn, i, 0, :, :half].astype(F32)
+            for y in range(1, n_y):
+                total = total + chip_sums[turn, i, y, :, :half].astype(F32)
+            if last:
+                score_half[i] = total * (1.0 / math.sqrt(samples))
+                here = score_out.at[:, pl.ds(pl.multiple_of(start + core * half, 128), half)]
+                copy = pltpu.make_async_copy(score_half.at[i], here, out_sem.at[1 + i])
+                copy.start()
+                outs.append(copy)
+                c_copies[i] = remote(
+                    score_half.at[i], here, c_send.at[turn, i], c_recv.at[turn, i], core_peer
                 )
-            i = t - LAG_A
-            if 0 <= i < count:
-                half = chunks[i][2] // 2
-                a_copies[i].wait_recv()
-                chip_sum = grad_bf[turn, i, core, :, :half].astype(F32) + from_core[
-                    turn, i, :, :half
-                ].astype(F32)
-                chip_sums[turn, i, y_at, :, :half] = chip_sum.astype(BF16)
-                here = chip_sums.at[turn, i, y_at, :, pl.ds(0, half)]
-                b_copies[i] = [
-                    remote(here, here, b_send.at[turn, i, d], b_recv.at[turn, i, d], peer)
-                    for d, peer in enumerate(y_peers)
-                ]
-            i = t - LAG_B
-            if 0 <= i < count:
-                ref, start, width = chunks[i]
-                half = width // 2
-                for copy in b_copies[i]:
-                    copy.wait_recv()
-                total = chip_sums[turn, i, 0, :, :half].astype(F32)
-                for y in range(1, n_y):
-                    total = total + chip_sums[turn, i, y, :, :half].astype(F32)
-                if last:
-                    score_half[i] = total * (1.0 / math.sqrt(samples))
-                    here = score_out.at[:, pl.ds(pl.multiple_of(start + core * half, 128), half)]
-                    copy = pltpu.make_async_copy(score_half.at[i], here, out_sem.at[1 + i])
-                    copy.start()
-                    outs.append(copy)
-                    c_copies[i] = remote(
-                        score_half.at[i], here, c_send.at[turn, i], c_recv.at[turn, i], core_peer
-                    )
+            else:
+                if turn > 0:
+                    before = coef_new[i, :, :half]
+                elif ref is admitted:
+                    before = jnp.zeros((traits.shape[0], half), F32)
                 else:
-                    if turn > 0:
-                        before = coef_new[i, :, :half]
-                    elif ref is admitted:
-                        before = jnp.zeros((traits.shape[0], half), F32)
-                    else:
-                        before = coef_start[:, pl.ds(pl.multiple_of(start + core * half, 128), half)]
-                    moved = before + scale * total
-                    after = moved - jnp.clip(moved, -threshold, threshold)
-                    coef_new[i, :, :half] = after
-                    coef_bf[turn, i, core, :, :half] = after.astype(BF16)
-                    here = coef_bf.at[turn, i, core, :, pl.ds(0, half)]
-                    c_copies[i] = remote(here, here, c_send.at[turn, i], c_recv.at[turn, i], core_peer)
-            i = t - LAG_C
-            if 0 <= i < count:
-                ref, start, width = chunks[i]
-                half = width // 2
-                c_copies[i].wait_recv()
-                if not last:
-                    fitted = fitted + dot_nt(coef_bf[turn, i, 0, :, :half], ref[:, start : start + half])
-                    fitted = fitted + dot_nt(
-                        coef_bf[turn, i, 1, :, :half], ref[:, start + half : start + width]
-                    )
+                    before = coef_start[:, pl.ds(pl.multiple_of(start + core * half, 128), half)]
+                moved = before + scale * total
+                after = moved - jnp.clip(moved, -threshold, threshold)
+                coef_new[i, :, :half] = after
+                coef_bf[turn, i, core, :, :half] = after.astype(BF16)
+                here = coef_bf.at[turn, i, core, :, pl.ds(0, half)]
+                c_copies[i] = remote(here, here, c_send.at[turn, i], c_recv.at[turn, i], core_peer)
+        for i in range(count):
+            ref, start, width = chunks[i]
+            half = width // 2
+            c_copies[i].wait_recv()
+            if not last:
+                fitted = fitted + dot_nt(coef_bf[turn, i, 0, :, :half], ref[:, start : start + half])
+                fitted = fitted + dot_nt(
+                    coef_bf[turn, i, 1, :, :half], ref[:, start + half : start + width]
+                )
         if not last:
             take_fit(turn + 1, send_fit(turn + 1, fitted))
 
@@ -247,6 +252,7 @@
     turns = ITERS + 1
     n_y = n_samp // 2
     any_spec = pl.BlockSpec(memory_space=pl.ANY)
+    hbm_spec = pl.BlockSpec(memory_space=pltpu.HBM)
     dma = pltpu.SemaphoreType.DMA
     return pl.pallas_call(
         functools.partial(kernel, (n_col, n_samp, samples, step_size)),
@@ -254,20 +260,21 @@
             jax.ShapeDtypeStruct(traits.shape, F32),
             jax.ShapeDtypeStruct((n_traits, CAND_DEV), F32),
         ),
-        in_specs=[any_spec] * 6,
+        in_specs=[hbm_spec] * 6,
         out_specs=(any_spec, any_spec),
         scratch_shapes=[
             pltpu.VMEM(dosage.shape, BF16),
             pltpu.VMEM(candidates.shape, BF16),
             pltpu.VMEM(traits.shape, F32),
             pltpu.VMEM(coef_start.shape, F32),
-            pltpu.VMEM((n_col, NEW_DEV), jnp.int32),
-            pltpu.VMEM((n_traits, 1), F32),
+            pltpu.VMEM(screened.shape, jnp.int32),
+            pltpu.VMEM(penalty.shape, F32),
             pltpu.VMEM((slots, CAND_DEV), BF16),
             pltpu.VMEM((rows, slots), BF16),
             pltpu.VMEM((chunks, n_traits, half), F32),
             pltpu.VMEM(traits.shape, F32),
             pltpu.VMEM(traits.shape, BF16),
+            pltpu.VMEM(traits.shape, F32),
             pltpu.VMEM((CAND_DEV // WIDE, n_traits, WIDE // 2), F32),
             pltpu.VMEM((turns, n_col) + traits.shape, BF16),
             pltpu.VMEM((turns, chunks, 2, n_traits, half), BF16),
@@ -288,11 +295,10 @@
             dma((turns, chunks)),
         ],
         compiler_params=pltpu.CompilerParams(
-            collective_id=0, has_side_effects=True, vmem_limit_bytes=50 * 1024 * 1024
+            collective_id=0, has_side_effects=True, vmem_limit_bytes=64 * 1024 * 1024
         ),
     )(
-        dosage, candidates, traits, coef_start,
-        screened.reshape(n_col, NEW_DEV), penalty.reshape(n_traits, 1),
+        dosage, candidates, traits, coef_start, screened, penalty
     )
 
 

time: 48.7 us -> 43.1 us (0.89)
  Pallas kernels: 43.3 us -> 39.2 us
  local copies, waits for them, and re-layouts: 4.48 us -> 3.04 us
    pallas_call x1, Pallas kernels: 43.3 us -> 39.2 us  [on_device(): pl.pallas_call(functools.partial(kernel, (n_col, n_samp, samples, step_si...]
    reshape x2 -> x0, local copies, waits for them, and re-layouts: 1.43 us -> none  [the longest x1 0.73 us: on_device(): penalty.reshape(n_traits, 1)]
    unnamed x6 -> x2, local copies, waits for them, and re-layouts: 3.05 us -> 3.04 us
where the time goes in v2:
time: 43.1 us; the launch traced here: 42.9 us
  Pallas kernels  39.2 us (91%)
  local copies, waits for them, and re-layouts  3.04 us (7%)
  between operations  0.64 us (1%)
    pallas_call x1, Pallas kernels, on_device(): pl.pallas_call(functools.partial(kernel, (n_col, n_samp, samples, step_si...  39.2 us
    unnamed x2, local copies, waits for them, and re-layouts  3.04 us

profile of v2, /device:TPU:0, one launch (start us, length us, event | category | flops | bytes accessed | tf_op | source)
XLA Modules:
  0.0 42.9 jit_solution(4665463892575353674)
XLA Ops:
  0.6 39.2 %shard_map.77 = (f32[16,512]{1,0:T(8,128)}, f32[16,4096]{1,0:T(8,128)}) custom-call(bf16[512,5120]{1,0:T(8,128)(2,1)} %dosage_hbm.1, bf16[512,4096]{1,0:T(8,128)(2,1)} %cand_hbm.1, f32[16,512]{1,0:T(8,128)} %traits_hbm.1, f32[16,5120]{1,0:T(8,128)} %coef_hbm.1, s32[1024]{0:T(1024)} %screened_hbm.1, f32[16]{0:T(128)} %penalty_hbm.1), custom_call_target="tpu_custom_call" | custom-call | tf_op jit(solution)/shard_map/pallas_call | solution.py:257
  39.8 1.4 %copy.10 = f32[16,512]{1,0:T(8,128)} copy(f32[16,512]{1,0:T(8,128)} %get-tuple-element.4) | data formatting | bytes 65536
  41.2 1.7 %copy.11 = f32[16,4096]{1,0:T(8,128)} copy(f32[16,4096]{1,0:T(8,128)} %get-tuple-element.5) | data formatting | bytes 524288

commit v3 on v2

--- a/solution.py
+++ b/solution.py
@@ -30,9 +30,9 @@
     dosage_hbm, cand_hbm, traits_hbm, coef_hbm, screened_hbm, penalty_hbm,
     resid_out, score_out,
     dosage, cand, traits, coef_start, screened, penalty,
-    one_hot, admitted, coef_new, resid_f32, resid_bf, sent, score_half,
+    one_hot, admitted, coef_new, resid_f32, resid_bf, sent,
     fit_slots, grad_bf, from_core, chip_sums, coef_bf,
-    load_sem, cand_sem, small_sem, out_sem,
+    load_sem, cand_sem, small_sem,
     fit_send, fit_recv, a_send, a_recv, b_send, b_recv, c_send, c_recv,
 ):
     n_col, n_samp, samples, step_size = sizes
@@ -162,9 +162,7 @@
         a_copies, b_copies, c_copies = {}, {}, {}
         fitted = jnp.zeros(traits.shape, F32)
         if last:
-            out_copy = pltpu.make_async_copy(resid_f32, resid_out, out_sem.at[0])
-            out_copy.start()
-        outs = []
+            resid_out[...] = resid_f32[...]
         resid = resid_bf[...]
         for t in range(count):
             ref, start, width = chunks[t]
@@ -198,14 +196,10 @@
             for y in range(1, n_y):
                 total = total + chip_sums[turn, i, y, :, :half].astype(F32)
             if last:
-                score_half[i] = total * (1.0 / math.sqrt(samples))
-                here = score_out.at[:, pl.ds(pl.multiple_of(start + core * half, 128), half)]
-                copy = pltpu.make_async_copy(score_half.at[i], here, out_sem.at[1 + i])
-                copy.start()
-                outs.append(copy)
-                c_copies[i] = remote(
-                    score_half.at[i], here, c_send.at[turn, i], c_recv.at[turn, i], core_peer
-                )
+                at = pl.ds(pl.multiple_of(start + core * half, 128), half)
+                score_out[:, at] = total * (1.0 / math.sqrt(samples))
+                here = score_out.at[:, at]
+                c_copies[i] = remote(here, here, c_send.at[turn, i], c_recv.at[turn, i], core_peer)
             else:
                 if turn > 0:
                     before = coef_new[i, :, :half]
@@ -231,9 +225,6 @@
         if not last:
             take_fit(turn + 1, send_fit(turn + 1, fitted))
 
-    out_copy.wait()
-    for copy in outs:
-        copy.wait()
     for copy in sends:
         copy.wait_send()
 
@@ -251,17 +242,17 @@
     half = max(WIDE, slots) // 2
     turns = ITERS + 1
     n_y = n_samp // 2
-    any_spec = pl.BlockSpec(memory_space=pl.ANY)
+    vmem_spec = pl.BlockSpec(memory_space=pltpu.VMEM)
     hbm_spec = pl.BlockSpec(memory_space=pltpu.HBM)
     dma = pltpu.SemaphoreType.DMA
     return pl.pallas_call(
         functools.partial(kernel, (n_col, n_samp, samples, step_size)),
         out_shape=(
-            jax.ShapeDtypeStruct(traits.shape, F32),
-            jax.ShapeDtypeStruct((n_traits, CAND_DEV), F32),
+            pltpu.VMEM(traits.shape, F32),
+            pltpu.VMEM((n_traits, CAND_DEV), F32),
         ),
         in_specs=[hbm_spec] * 6,
-        out_specs=(any_spec, any_spec),
+        out_specs=(vmem_spec, vmem_spec),
         scratch_shapes=[
             pltpu.VMEM(dosage.shape, BF16),
             pltpu.VMEM(candidates.shape, BF16),
@@ -275,7 +266,6 @@
             pltpu.VMEM(traits.shape, F32),
             pltpu.VMEM(traits.shape, BF16),
             pltpu.VMEM(traits.shape, F32),
-            pltpu.VMEM((CAND_DEV // WIDE, n_traits, WIDE // 2), F32),
             pltpu.VMEM((turns, n_col) + traits.shape, BF16),
             pltpu.VMEM((turns, chunks, 2, n_traits, half), BF16),
             pltpu.VMEM((turns, chunks, n_traits, half), BF16),
@@ -284,7 +274,6 @@
             dma((active // WIDE,)),
             dma((1,)),
             dma((4,)),
-            dma((1 + CAND_DEV // WIDE,)),
             dma((turns, n_col - 1)),
             dma((turns, n_col - 1)),
             dma((turns, chunks)),
@@ -295,10 +284,13 @@
             dma((turns, chunks)),
         ],
         compiler_params=pltpu.CompilerParams(
-            collective_id=0, has_side_effects=True, vmem_limit_bytes=64 * 1024 * 1024
+            collective_id=0, has_side_effects=True, vmem_limit_bytes=50 * 1024 * 1024
         ),
     )(
-        dosage, candidates, traits, coef_start, screened, penalty
+        *(
+            pltpu.with_memory_space_constraint(arg, pltpu.HBM)
+            for arg in (dosage, candidates, traits, coef_start, screened, penalty)
+        )
     )
 
 

time: 43.1 us -> 41.1 us (0.954)
  local copies, waits for them, and re-layouts: 3.04 us -> 1.32 us
    unnamed x2, local copies, waits for them, and re-layouts: 3.04 us -> 1.32 us
where the time goes in v3:
time: 41.1 us; the launch traced here: 41 us
  Pallas kernels  39 us (95%)
  local copies, waits for them, and re-layouts  1.32 us (3%)
  between operations  0.64 us (2%)
    pallas_call x1, Pallas kernels, on_device(): pl.pallas_call(functools.partial(kernel, (n_col, n_samp, samples, step_si...  39 us
    unnamed x2, local copies, waits for them, and re-layouts  1.32 us

profile of v3, /device:TPU:0, one launch (start us, length us, event | category | flops | bytes accessed | tf_op | source)
XLA Modules:
  0.0 41.0 jit_solution(15730455079482538650)
XLA Ops:
  0.6 39.0 %shard_map.77 = (f32[16,512]{1,0:T(8,128)S(1)}, f32[16,4096]{1,0:T(8,128)S(1)}) custom-call(bf16[512,5120]{1,0:T(8,128)(2,1)} %dosage_hbm.1, bf16[512,4096]{1,0:T(8,128)(2,1)} %cand_hbm.1, f32[16,512]{1,0:T(8,128)} %traits_hbm.1, f32[16,5120]{1,0:T(8,128)} %coef_hbm.1, s32[1024]{0:T(1024)} %screened_hbm.1, f32[16]{0:T(128)} %penalty_hbm.1), custom_call_target="tpu_custom_call" | custom-call | tf_op jit(solution)/shard_map/pallas_call | solution.py:248
  39.6 0.6 %copy.10 = f32[16,512]{1,0:T(8,128)} copy(f32[16,512]{1,0:T(8,128)S(1)} %get-tuple-element.2) | data formatting | bytes 65536
  40.3 0.7 %copy.11 = f32[16,4096]{1,0:T(8,128)} copy(f32[16,4096]{1,0:T(8,128)S(1)} %get-tuple-element.3) | data formatting | bytes 524288
